TPU v7x, 256 devices: a whole 4x4x8 slice. The times are simulated.
256 devices in a mesh: dp: 16 (over z, core), context: 4 (over y), tensor: 4 (over x).
Axes of the slice: x: 4, y: 4, z: 8, core: 2. Of those that a mesh axis runs over, the one named last changes fastest.
Arguments:
- queries: bfloat16 [49152, 2048], P(('dp', 'context', 'tensor')), parts along dimension 0, may hold values from -112 to 112
- keys: bfloat16 [49152, 2048], P(('dp', 'context', 'tensor')), parts along dimension 0, may hold values from -4 to 4
- values: bfloat16 [49152, 2048], P(('dp', 'context', 'tensor')), parts along dimension 0, may hold values from -6 to 6
- doc_ids: int32 [49152], P('dp'), parts along dimension 0, may hold values from 0 to 2, never falling along the last dimension, each value on 1 to 1536 neighbouring positions
- span_lo: int32 [96], P('dp'), parts along dimension 0, may hold values from 0 to 3071, as said below
- span_hi: int32 [96], P('dp'), parts along dimension 0, may hold values from 1 to 3072, as said below
Outputs:
- attended: bfloat16 [49152, 2048], P(('dp', 'context', 'tensor')), parts along dimension 0
There are 16 independent parts, one for each index of `dp`. A program takes and returns all parts, laid end to end along the dimension named above; each array names one. Nothing has to cross between parts.
Inputs may be any that keep to these rules, and one draw needn't show every extreme that they name: `span_lo`: spans are disjoint; span s lies within positions s * 512 to (s + 1) * 512 - 1 and is 128 to 256 long. span_hi[s] > span_lo[s] for every span. `doc_ids`: document ids never fall along the slab.
All inputs are finite; a program needn't handle non-finite values.
Results may differ from a plain program's by a relative error of at most 0.0049.
Values may be sent and summed in bfloat16 or wider, within the bound.
A program may use at most 128 MiB of HBM per device.

v0:
```python
import jax
import jax.numpy as jnp
from jax import lax
from jax.sharding import PartitionSpec as P

D_HEAD = 128


def span_image(span_lo, span_hi, positions):
    inside = (positions[:, None] >= span_lo[None, :]) & (positions[:, None] < span_hi[None, :])
    number = jnp.arange(span_lo.shape[0], dtype=jnp.int32)[None, :] + 1
    image = jnp.sum(jnp.where(inside, number, 0), axis=1) - 1
    further = jnp.sum(jnp.where(inside, span_hi[None, :] - 1 - positions[:, None], 0), axis=1)
    return (image, positions + further)


def attend(q_local, qstart, doc_ids, span_lo, span_hi, folder):
    qrows = q_local.shape[0]
    heads = q_local.shape[1] // D_HEAD
    scale = 1.0 / D_HEAD**0.5
    qsplit = q_local.reshape(qrows, heads, D_HEAD)
    qpos = qstart + jnp.arange(qrows, dtype=jnp.int32)
    qdoc = lax.dynamic_slice_in_dim(doc_ids, qstart, qrows)
    qimage, qreach = span_image(span_lo, span_hi, qpos)

    def update(carry, kblock, vblock, kstart):
        top, total, summed = carry
        width = kblock.shape[0]
        ksplit = kblock.reshape(width, heads, D_HEAD)
        vsplit = vblock.reshape(width, heads, D_HEAD)
        kpos = kstart + jnp.arange(width, dtype=jnp.int32)
        kdoc = lax.dynamic_slice_in_dim(doc_ids, kstart, width)
        kimage, unused = span_image(span_lo, span_hi, kpos)
        allowed = (qdoc[:, None] == kdoc[None, :]) & (
            (kpos[None, :] <= qpos[:, None])
            | (qimage[:, None] == kimage[None, :]) & (qimage[:, None] >= 0)
        )
        scores = (
            jnp.einsum("qhd,khd->hqk", qsplit, ksplit, preferred_element_type=jnp.float32) * scale
        )
        scores = jnp.where(allowed[None], scores, -1e30)
        new_top = jnp.maximum(top, jnp.max(scores, axis=2))
        weights = jnp.where(allowed[None], jnp.exp(scores - new_top[..., None]), 0.0)
        factor = jnp.exp(top - new_top)
        total = factor * total + jnp.sum(weights, axis=2)
        summed = factor[..., None] * summed + jnp.einsum(
            "hqk,khd->hqd", weights.astype(jnp.bfloat16), vsplit, preferred_element_type=jnp.float32
        )
        return (new_top, total, summed)

    def fold_piece(carry, piece, start):
        kpiece, vpiece = piece
        count = kpiece.shape[0]
        block = 512
        nblocks = count // block
        kblocks = kpiece.reshape(nblocks, block, kpiece.shape[1])
        vblocks = vpiece.reshape(nblocks, block, vpiece.shape[1])
        starts = block * jnp.arange(nblocks, dtype=jnp.int32)

        def step(state, item):
            kblock, vblock, kstart = item
            state = update(state, kblock, vblock, kstart)
            return (state, None)

        carry, unused = lax.scan(step, carry, (kblocks, vblocks, starts))
        return carry

    init = (
        jnp.full((heads, qrows), -1e30, jnp.float32),
        jnp.zeros((heads, qrows), jnp.float32),
        jnp.zeros((heads, qrows, D_HEAD), jnp.float32),
    )
    top, total, summed = folder(fold_piece, init)
    result = summed / total[..., None]
    return result.transpose(1, 0, 2).reshape(qrows, heads * D_HEAD).astype(jnp.bfloat16)


def per_device(queries, keys, values, doc_ids, span_lo, span_hi):
    rows = queries.shape[0]
    qstart = lax.axis_index(("context", "tensor")) * rows

    def folder(fold_piece, init):
        return fold_piece(
            init,
            (
                lax.all_gather(keys, ("context", "tensor"), axis=0, tiled=True),
                lax.all_gather(values, ("context", "tensor"), axis=0, tiled=True),
            ),
            jnp.int32(0),
        )

    return attend(queries, qstart, doc_ids, span_lo, span_hi, folder)


def solution(mesh):
    placed = (
        P(("dp", "context", "tensor"), None),
        P(("dp", "context", "tensor"), None),
        P(("dp", "context", "tensor"), None),
        P("dp"),
        P("dp"),
        P("dp"),
    )
    return jax.shard_map(
        per_device,
        mesh=mesh,
        in_specs=placed,
        out_specs=P(("dp", "context", "tensor"), None),
        check_vma=False,
    )
```

profile of v0, /device:TPU:32, one launch (start us, length us, event | category | flops | bytes accessed | tf_op | source)
XLA Modules:
  0.0 358.3 jit_solution(4917950851035589788)
XLA Ops:
  10.7 96.7 %all-gather.3.cloned.1.call-done = bf16[3072,2048]{1,0:T(8,128)(2,1)} async-done(((bf16[192,2048]{1,0:T(8,128)(2,1)}), bf16[3072,2048]{1,0:T(8,128)(2,1)}) %all-gather.3.cloned.1.call-update) | async-done | bytes 12582928 | tf_op jit(solution)/shard_map/all_gather | solution.py:86
  107.5 97.2 %all-gather.5.cloned.1.call-done = bf16[3072,2048]{1,0:T(8,128)(2,1)} async-done(((bf16[192,2048]{1,0:T(8,128)(2,1)}), bf16[3072,2048]{1,0:T(8,128)(2,1)}) %all-gather.5.cloned.1.call-update) | async-done | bytes 12582928 | tf_op jit(solution)/shard_map/all_gather | solution.py:87
  204.7 144.0 %while.17 = (s32[]{:T(128)}, f32[16,192]{1,0:T(8,128)S(1)}, f32[16,192]{1,0:T(8,128)S(1)}, f32[16,192,128]{2,1,0:T(8,128)}, s32[192]{0:T(256)S(1)}, /*index=5*/s...) while((s32[]{:T(128)}, f32[16,192]{1,0:T(8,128)S(1)}, ...), condition=%wide.region_5.6_spmd.clone, body=%wide.region_1.5_spmd.clone.sunk | while | flops 827554688 | bytes 65364512 | solution.py:65
  208.6 4.8 %constant_dynamic-slice_fusion.3 = (bf16[1,512,2048]{2,1,0:T(8,128)(2,1)}, bf16[1,512,2048]{2,1,0:T(8,128)(2,1)}) fusion(bf16[6,512,2048]{2,1,0:T(8,128)(2,1)} %get-tuple-element.448, s32[]{:T(128)S(6)} %copy.40, bf16[6,512,2048]{2,1,0:T(8,128)(2,1)} %get-tuple-element.446), kind=kLoop, calls=%fused_computation.25.clone.1 | loop fusion | bytes 8388612 | tf_op jit(solution)/shard_map/while/body/jit(dynamic_index_in_dim)/dynamic_slice | solution.py:65
  213.3 2.9 copy.34
  216.2 3.9 %copy.35 = bf16[1,512,2048]{1,2,0:T(8,128)(2,1)} copy(bf16[1,512,2048]{2,1,0:T(8,128)(2,1)} %get-tuple-element.400) | data formatting | bytes 4194304 | tf_op jit(solution)/shard_map/while/body/jit(dynamic_index_in_dim)/dynamic_slice | solution.py:65
  224.8 2.7 fusion.40
  232.6 4.8 %constant_dynamic-slice_fusion.3 = (bf16[1,512,2048]{2,1,0:T(8,128)(2,1)}, bf16[1,512,2048]{2,1,0:T(8,128)(2,1)}) fusion(bf16[6,512,2048]{2,1,0:T(8,128)(2,1)} %get-tuple-element.448, s32[]{:T(128)S(6)} %copy.40, bf16[6,512,2048]{2,1,0:T(8,128)(2,1)} %get-tuple-element.446), kind=kLoop, calls=%fused_computation.25.clone.1 | loop fusion | bytes 8388612 | tf_op jit(solution)/shard_map/while/body/jit(dynamic_index_in_dim)/dynamic_slice | solution.py:65
  237.3 2.9 copy.34
  240.2 3.9 %copy.35 = bf16[1,512,2048]{1,2,0:T(8,128)(2,1)} copy(bf16[1,512,2048]{2,1,0:T(8,128)(2,1)} %get-tuple-element.400) | data formatting | bytes 4194304 | tf_op jit(solution)/shard_map/while/body/jit(dynamic_index_in_dim)/dynamic_slice | solution.py:65
  248.8 2.7 fusion.40
  256.5 4.8 %constant_dynamic-slice_fusion.3 = (bf16[1,512,2048]{2,1,0:T(8,128)(2,1)}, bf16[1,512,2048]{2,1,0:T(8,128)(2,1)}) fusion(bf16[6,512,2048]{2,1,0:T(8,128)(2,1)} %get-tuple-element.448, s32[]{:T(128)S(6)} %copy.40, bf16[6,512,2048]{2,1,0:T(8,128)(2,1)} %get-tuple-element.446), kind=kLoop, calls=%fused_computation.25.clone.1 | loop fusion | bytes 8388612 | tf_op jit(solution)/shard_map/while/body/jit(dynamic_index_in_dim)/dynamic_slice | solution.py:65
  261.3 2.9 copy.34
  264.2 3.9 %copy.35 = bf16[1,512,2048]{1,2,0:T(8,128)(2,1)} copy(bf16[1,512,2048]{2,1,0:T(8,128)(2,1)} %get-tuple-element.400) | data formatting | bytes 4194304 | tf_op jit(solution)/shard_map/while/body/jit(dynamic_index_in_dim)/dynamic_slice | solution.py:65
  268.1 2.5 fusion.37
  272.8 2.7 fusion.40
  280.6 4.8 %constant_dynamic-slice_fusion.3 = (bf16[1,512,2048]{2,1,0:T(8,128)(2,1)}, bf16[1,512,2048]{2,1,0:T(8,128)(2,1)}) fusion(bf16[6,512,2048]{2,1,0:T(8,128)(2,1)} %get-tuple-element.448, s32[]{:T(128)S(6)} %copy.40, bf16[6,512,2048]{2,1,0:T(8,128)(2,1)} %get-tuple-element.446), kind=kLoop, calls=%fused_computation.25.clone.1 | loop fusion | bytes 8388612 | tf_op jit(solution)/shard_map/while/body/jit(dynamic_index_in_dim)/dynamic_slice | solution.py:65
  285.3 2.9 copy.34
  288.2 3.9 %copy.35 = bf16[1,512,2048]{1,2,0:T(8,128)(2,1)} copy(bf16[1,512,2048]{2,1,0:T(8,128)(2,1)} %get-tuple-element.400) | data formatting | bytes 4194304 | tf_op jit(solution)/shard_map/while/body/jit(dynamic_index_in_dim)/dynamic_slice | solution.py:65
  292.1 2.5 fusion.37
  296.8 2.7 fusion.40
  304.6 4.8 %constant_dynamic-slice_fusion.3 = (bf16[1,512,2048]{2,1,0:T(8,128)(2,1)}, bf16[1,512,2048]{2,1,0:T(8,128)(2,1)}) fusion(bf16[6,512,2048]{2,1,0:T(8,128)(2,1)} %get-tuple-element.448, s32[]{:T(128)S(6)} %copy.40, bf16[6,512,2048]{2,1,0:T(8,128)(2,1)} %get-tuple-element.446), kind=kLoop, calls=%fused_computation.25.clone.1 | loop fusion | bytes 8388612 | tf_op jit(solution)/shard_map/while/body/jit(dynamic_index_in_dim)/dynamic_slice | solution.py:65
  309.3 2.9 copy.34
  312.2 3.9 %copy.35 = bf16[1,512,2048]{1,2,0:T(8,128)(2,1)} copy(bf16[1,512,2048]{2,1,0:T(8,128)(2,1)} %get-tuple-element.400) | data formatting | bytes 4194304 | tf_op jit(solution)/shard_map/while/body/jit(dynamic_index_in_dim)/dynamic_slice | solution.py:65
  316.1 2.5 fusion.37
  320.8 2.7 fusion.40
  328.6 4.8 %constant_dynamic-slice_fusion.3 = (bf16[1,512,2048]{2,1,0:T(8,128)(2,1)}, bf16[1,512,2048]{2,1,0:T(8,128)(2,1)}) fusion(bf16[6,512,2048]{2,1,0:T(8,128)(2,1)} %get-tuple-element.448, s32[]{:T(128)S(6)} %copy.40, bf16[6,512,2048]{2,1,0:T(8,128)(2,1)} %get-tuple-element.446), kind=kLoop, calls=%fused_computation.25.clone.1 | loop fusion | bytes 8388612 | tf_op jit(solution)/shard_map/while/body/jit(dynamic_index_in_dim)/dynamic_slice | solution.py:65
  333.3 2.9 copy.34
  336.2 3.9 %copy.35 = bf16[1,512,2048]{1,2,0:T(8,128)(2,1)} copy(bf16[1,512,2048]{2,1,0:T(8,128)(2,1)} %get-tuple-element.400) | data formatting | bytes 4194304 | tf_op jit(solution)/shard_map/while/body/jit(dynamic_index_in_dim)/dynamic_slice | solution.py:65
  340.1 2.5 fusion.37
  344.8 2.7 fusion.40
  348.7 2.8 copy_bitcast_fusion
  (136 shorter events, 41.9 us)
Async XLA Ops:
  6.5 3.1 copy-start
  6.5 198.1 %copy-start.4 = (s32[6]{0:T(128)S(1)}, s32[6]{0:T(128)}, u32[]{:S(2)}) copy-start(s32[6]{0:T(128)} %param.13) | copy-start | bytes 76
  6.5 198.1 %copy-start.5 = (s32[6]{0:T(128)S(1)}, s32[6]{0:T(128)}, u32[]{:S(2)}) copy-start(s32[6]{0:T(128)} %param.12) | copy-start | bytes 76
  6.5 100.9 %all-gather.3.cloned.1.call-start = ((), (), s32[]{:S(2)}) async-start(), calls=%async_computation | async-start | bytes 13369344 | tf_op jit(solution)/shard_map/all_gather | solution.py:86
  7.3 197.4 %all-gather.5.cloned.1.call-start = ((), (), s32[]{:S(2)}) async-start(), calls=%async_computation.1 | async-start | bytes 13369344 | tf_op jit(solution)/shard_map/all_gather | solution.py:87
  222.7 2.1 copy-start.1
  222.7 2.1 copy-start.2
  227.5 1.2 copy-start.3
  246.7 2.1 copy-start.1
  246.7 2.1 copy-start.2
  251.5 1.2 copy-start.3
  270.7 2.1 copy-start.1
  270.7 2.1 copy-start.2
  275.5 1.2 copy-start.3
  294.7 2.1 copy-start.1
  294.7 2.1 copy-start.2
  299.5 1.2 copy-start.3
  318.7 2.1 copy-start.1
  318.7 2.1 copy-start.2
  323.5 1.2 copy-start.3
  342.7 2.1 copy-start.1
  342.7 2.1 copy-start.2
  347.5 1.2 copy-start.3
Sparse Core Ops, SparseCore 0:
  9.8 97.6 all-gather.2
  109.9 94.7 all-gather.4
where the time goes:
time: 361 us; the launch traced here: 358 us
  waiting for transfers between devices  195 us (54%)
  local copies, waits for them, and re-layouts  86.2 us (24%)
  matrix products  31.4 us (9%)
  other arithmetic  21.2 us (6%)
  between operations  13.5 us (4%)
  loops' own time  10.6 us (3%)
    all_gather x1, waiting for transfers between devices, folder(): lax.all_gather(values, ('context', 'tensor'), axis=0, tiled=True)  97.2 us
    all_gather x1, waiting for transfers between devices, folder(): lax.all_gather(keys, ('context', 'tensor'), axis=0, tiled=True)  96.7 us
    dynamic_slice x24, local copies, waits for them, and re-layouts, fold_piece(): carry, unused = lax.scan(step, carry, (kblocks, vblocks, starts))  72.6 us
    dot_general x6, matrix products, update(): jnp.einsum('hqk,khd->hqd', weights.astype(jnp.bfloat16), vsplit, preferre...  16.2 us
    dot_general x6, matrix products, update(): jnp.einsum('qhd,khd->hqk', qsplit, ksplit, preferred_element_type=jnp.flo...  15.2 us
    reduce_sum x6, other arithmetic, update(): total = factor * total + jnp.sum(weights, axis=2)  12.3 us
    another operation x1, loops' own time, fold_piece(): carry, unused = lax.scan(step, carry, (kblocks, vblocks, starts))  10.6 us
  transfers between devices with their start and end apart: 2, of which 2 were waited for; matrix products, arithmetic and copies ran while one was open for 1% of the time, Pallas kernels for 0%

commit v1 on v0

v1 whole, which is shorter than its diff:
```python
import functools

import jax
import jax.numpy as jnp
from jax import lax
from jax.experimental import pallas as pl
from jax.experimental.pallas import tpu as pltpu
from jax.sharding import PartitionSpec as P

MESH = pl.DeviceIdType.MESH
D = 128
LOG2E = 1.4426950408889634
BLOCK = 256
BACK = 64
REACH = 6
FAR = float(2**20)


def kernel(
    nc, nt, q_hbm, k_hbm, v_hbm, docs_hbm, lo_hbm, hi_hbm, out,
    qb, kb, vb, rb, ob, sb, docs, lo, hi, ssem, rsem, osend, orecv, lsem,
):
    rows = q_hbm.shape[0]
    n = nc * nt
    slab = n * rows
    front = kb.shape[0] - slab - 256
    c, t = lax.axis_index("context"), lax.axis_index("tensor")
    me = c * nt + t

    def device(rank):
        return {"context": rank // nt, "tensor": rank % nt}

    def ahead(i):
        return ((c + i // nt) % nc) * nt + (t + i % nt) % nt

    def behind(i):
        return ((c + nc - i // nt) % nc) * nt + (t + nt - i % nt) % nt

    barrier = pltpu.get_barrier_semaphore()
    for i in range(1, n):
        pl.semaphore_signal(barrier, inc=1, device_id=device(ahead(i)), device_id_type=MESH)
    pl.semaphore_wait(barrier, n - 1)

    sources = (k_hbm, v_hbm, q_hbm)
    buffers = (kb, vb, qb)
    offsets = (front, front, 0)

    def columns(rank):
        return pl.ds(pl.multiple_of(rank * D, D), D)

    def place(a, rank):
        return buffers[a].at[pl.ds(pl.multiple_of(offsets[a] + rank * rows, 64), rows), pl.ds(0, D)]

    def send(a, i):
        to = ahead(i)
        return pltpu.make_async_remote_copy(
            src_ref=sources[a].at[:, columns(to)],
            dst_ref=place(a, me),
            send_sem=ssem.at[a, i],
            recv_sem=rsem.at[a, i],
            device_id=device(to),
            device_id_type=MESH,
        )

    def own(a):
        return pltpu.make_async_copy(sources[a].at[:, columns(me)], place(a, me), lsem.at[a])

    small = [
        pltpu.make_async_copy(docs_hbm, docs, lsem.at[3]),
        pltpu.make_async_copy(lo_hbm, lo, lsem.at[4]),
        pltpu.make_async_copy(hi_hbm, hi, lsem.at[5]),
    ]
    for a in range(3):
        for i in range(1, n):
            send(a, i).start()
        own(a).start()
        if a == 0:
            for copy in small:
                copy.start()
    for copy in small:
        copy.wait()

    lane = lax.broadcasted_iota(jnp.int32, (D, D), 1)
    row = lax.broadcasted_iota(jnp.int32, (D, D), 0)
    for b in range(slab // D):
        doc = jnp.transpose(jnp.broadcast_to(docs[b : b + 1, :], (D, D)))
        same = doc == lane
        kb[front + b * D : front + (b + 1) * D, D:] = jnp.where(same, 1.0, 0.0).astype(jnp.bfloat16)
        qb[b * D : (b + 1) * D, D:] = jnp.where(same | (lane > 2), 0.0, -FAR).astype(jnp.bfloat16)
        at = row + b * D
        last = at
        for s in range(lo_hbm.shape[0]):
            last = jnp.where((at >= lo[s]) & (at < hi[s]), hi[s] - 1, last)
        rb[b * D : (b + 1) * D, :] = last
    for start, count in ((0, front), (front + slab, 256)):
        kb[start : start + count, :D] = jnp.zeros((count, D), jnp.bfloat16)
        kb[start : start + count, D:] = jnp.ones((count, D), jnp.bfloat16)
        vb[start : start + count, :D] = jnp.zeros((count, D), jnp.bfloat16)
    vb[:, D:] = jnp.ones((vb.shape[0], D), jnp.bfloat16)

    for a in range(2):
        own(a).wait()
        for i in range(1, n):
            send(a, i).wait_recv()
    own(2).wait()

    factor = LOG2E / D**0.5

    def answer(i, rank):
        return pltpu.make_async_remote_copy(
            src_ref=ob.at[pl.ds(pl.multiple_of(rank * rows, 64), rows), :],
            dst_ref=out.at[:, columns(me)],
            send_sem=osend.at[i],
            recv_sem=orecv.at[i],
            device_id=device(rank),
            device_id_type=MESH,
        )

    def keep():
        return pltpu.make_async_copy(
            ob.at[pl.ds(pl.multiple_of(me * rows, 64), rows), :], out.at[:, columns(me)], lsem.at[6]
        )

    def chunk(i, carry):
        @pl.when(i > 0)
        def _():
            send(2, i).wait_recv()

        rank = behind(i)
        q0 = pl.multiple_of(rank * rows, 64)
        count = jnp.minimum((3 * rank + 2) // 4, REACH)
        base = front + q0 - BACK - BLOCK * count
        qa = qb[pl.ds(q0, rows), :]

        def score(j):
            kj = kb[pl.ds(pl.multiple_of(base + BLOCK * j, 64), BLOCK), :]
            return lax.dot_general(qa, kj, (((1,), (1,)), ((), ())), preferred_element_type=jnp.float32)

        def first(j, top):
            x = score(j)
            sb[j] = x
            return jnp.maximum(top, jnp.maximum(x[:, :D], x[:, D:]))

        top = lax.fori_loop(0, count, first, jnp.full((rows, D), -3e38, jnp.float32))
        limit = rb[pl.ds(q0, rows), :] - (q0 - BACK)
        column = lax.broadcasted_iota(jnp.int32, (rows, D), 1)
        for part in range(2):
            x = score(count + part)
            for half in range(2):
                xh = x[:, half * D : (half + 1) * D]
                xh = jnp.where(column + (part * BLOCK + half * D) <= limit, xh, -1e30)
                sb[count + part, :, half * D : (half + 1) * D] = xh
                top = jnp.maximum(top, xh)
        top = jnp.max(top, axis=1, keepdims=True)

        def second(j, total):
            p = jnp.exp2((sb[j] - top) * factor).astype(jnp.bfloat16)
            vj = vb[pl.ds(pl.multiple_of(base + BLOCK * j, 64), BLOCK), :]
            return total + jnp.dot(p, vj, preferred_element_type=jnp.float32)

        total = lax.fori_loop(0, count + 2, second, jnp.zeros((rows, 2 * D), jnp.float32))
        ob[pl.ds(q0, rows), :] = (total[:, :D] / total[:, D:]).astype(jnp.bfloat16)

        @pl.when(i > 0)
        def _():
            answer(i, rank).start()

        @pl.when(i == 0)
        def _():
            keep().start()

        return carry

    lax.fori_loop(0, n, chunk, 0)

    keep().wait()
    for i in range(1, n):
        answer(i, behind(i)).wait_recv()
    for i in range(1, n):
        answer(i, behind(i)).wait_send()
    for a in range(3):
        for i in range(1, n):
            send(a, i).wait_send()


def solution(mesh):
    nc, nt = mesh.shape["context"], mesh.shape["tensor"]
    n = nc * nt

    def step(queries, keys, values, doc_ids, span_lo, span_hi):
        rows, width = queries.shape
        slab = doc_ids.shape[0]
        spans = span_lo.shape[0]
        padded = 192 + slab + 256
        bf16, f32, i32 = jnp.bfloat16, jnp.float32, jnp.int32
        return pl.pallas_call(
            functools.partial(kernel, nc, nt),
            out_shape=jax.ShapeDtypeStruct((rows, width), bf16),
            in_specs=[pl.BlockSpec(memory_space=pltpu.HBM)] * 6,
            out_specs=pl.BlockSpec(memory_space=pltpu.HBM),
            scratch_shapes=[
                pltpu.VMEM((slab, 2 * D), bf16),
                pltpu.VMEM((padded, 2 * D), bf16),
                pltpu.VMEM((padded, 2 * D), bf16),
                pltpu.VMEM((slab, D), i32),
                pltpu.VMEM((slab, D), bf16),
                pltpu.VMEM((REACH + 2, rows, BLOCK), f32),
                pltpu.VMEM((slab // D, D), i32),
                pltpu.SMEM((spans,), i32),
                pltpu.SMEM((spans,), i32),
                pltpu.SemaphoreType.DMA((3, n)),
                pltpu.SemaphoreType.DMA((3, n)),
                pltpu.SemaphoreType.DMA((n,)),
                pltpu.SemaphoreType.DMA((n,)),
                pltpu.SemaphoreType.DMA((7,)),
            ],
            compiler_params=pltpu.CompilerParams(
                collective_id=0, has_side_effects=True, vmem_limit_bytes=63 << 20
            ),
        )(queries, keys, values, doc_ids.reshape(slab // D, D), span_lo, span_hi)

    rows = P(("dp", "context", "tensor"), None)
    return jax.shard_map(
        step,
        mesh=mesh,
        in_specs=(rows, rows, rows, P("dp"), P("dp"), P("dp")),
        out_specs=rows,
        check_vma=False,
    )
```

time: 361 us -> 77.7 us (0.22)
  waiting for transfers between devices: 195 us -> 0 us
  local copies, waits for them, and re-layouts: 86.2 us -> 2.09 us
  Pallas kernels: 0 us -> 75.4 us
  matrix products: 31.4 us -> 0 us
  other arithmetic: 21.2 us -> 0 us
  between operations: 13.5 us -> 0.01 us
  loops' own time: 10.6 us -> 0 us
    all_gather x2 -> x0, waiting for transfers between devices: 194 us -> none  [the longest x1 97.2 us: folder(): lax.all_gather(values, ('context', 'tensor'), axis=0, tiled=True)]
    dynamic_slice x31 -> x0, local copies, waits for them, and re-layouts: 78 us -> none  [the longest x24 72.6 us: fold_piece(): carry, unused = lax.scan(step, carry, (kblocks, vblocks, starts))]
    pallas_call x0 -> x1, Pallas kernels: none -> 75.4 us  [step(): pl.pallas_call(functools.partial(kernel, nc, nt), out_shape=jax.ShapeDtyp...]
    dot_general x12 -> x0, matrix products: 31.4 us -> none  [the longest x6 16.2 us: update(): jnp.einsum('hqk,khd->hqd', weights.astype(jnp.bfloat16), vsplit, preferre...]
    reduce_sum x13 -> x0, other arithmetic: 13.6 us -> none  [the longest x6 12.3 us: update(): total = factor * total + jnp.sum(weights, axis=2)]
    another operation x1 -> x0, loops' own time: 10.6 us -> none  [fold_piece(): carry, unused = lax.scan(step, carry, (kblocks, vblocks, starts))]
    while x42 -> x0, local copies, waits for them, and re-layouts: 7.13 us -> none
  transfers between devices with their start and end apart: 2 -> 0, of which waited for: 2 -> 0; matrix products, arithmetic and copies ran while one was open for 1% -> 0% of each run, Pallas kernels for 0% -> 0%
where the time goes in v1:
time: 77.7 us; the launch traced here: 77.5 us
  Pallas kernels  75.4 us (97%)
  local copies, waits for them, and re-layouts  2.09 us (3%)
    pallas_call x1, Pallas kernels, step(): pl.pallas_call(functools.partial(kernel, nc, nt), out_shape=jax.ShapeDtyp...  75.4 us
    unnamed x1, local copies, waits for them, and re-layouts  2.09 us

profile of v1, /device:TPU:32, one launch (start us, length us, event | category | flops | bytes accessed | tf_op | source)
XLA Modules:
  0.0 77.5 jit_solution(10125602681650001386)
XLA Ops:
  0.0 75.4 %shard_map.64 = bf16[192,2048]{1,0:T(8,128)(2,1)} custom-call(bf16[192,2048]{1,0:T(8,128)(2,1)} %q_hbm.1, bf16[192,2048]{1,0:T(8,128)(2,1)} %k_hbm.1, bf16[192,2048]{1,0:T(8,128)(2,1)} %v_hbm.1, s32[24,128]{1,0:T(8,128)} %bitcast.1, s32[6]{0:T(128)} %lo_hbm.1, s32[6]{0:T(128)} %hi_hbm.1), custom_call_target="tpu_custom_call" | custom-call | tf_op jit(solution)/shard_map/pallas_call | solution.py:196
  75.4 2.1 %copy.8 = bf16[192,2048]{1,0:T(8,128)(2,1)} copy(bf16[192,2048]{1,0:T(8,128)(2,1)} %shard_map.64) | data formatting | bytes 1572864

commit v2 on v1

--- a/solution.py
+++ b/solution.py
@@ -18,12 +18,12 @@
 
 def kernel(
     nc, nt, q_hbm, k_hbm, v_hbm, docs_hbm, lo_hbm, hi_hbm, out,
-    qb, kb, vb, rb, ob, sb, docs, lo, hi, ssem, rsem, osend, orecv, lsem,
+    qb, kb, vb, rb, ob, sa, sb, tops, docs, lo, hi, ssem, rsem, osend, orecv, lsem,
 ):
     rows = q_hbm.shape[0]
     n = nc * nt
     slab = n * rows
-    front = kb.shape[0] - slab - 256
+    front = BACK + BLOCK * REACH
     c, t = lax.axis_index("context"), lax.axis_index("tensor")
     me = c * nt + t
 
@@ -92,7 +92,7 @@
         for s in range(lo_hbm.shape[0]):
             last = jnp.where((at >= lo[s]) & (at < hi[s]), hi[s] - 1, last)
         rb[b * D : (b + 1) * D, :] = last
-    for start, count in ((0, front), (front + slab, 256)):
+    for start, count in ((0, front), (front + slab, BLOCK)):
         kb[start : start + count, :D] = jnp.zeros((count, D), jnp.bfloat16)
         kb[start : start + count, D:] = jnp.ones((count, D), jnp.bfloat16)
         vb[start : start + count, :D] = jnp.zeros((count, D), jnp.bfloat16)
@@ -121,57 +121,69 @@
             ob.at[pl.ds(pl.multiple_of(me * rows, 64), rows), :], out.at[:, columns(me)], lsem.at[6]
         )
 
-    def chunk(i, carry):
-        @pl.when(i > 0)
+    column = lax.broadcasted_iota(jnp.int32, (rows, D), 1)
+
+    def key_rows(rank, j):
+        start = front + rank * rows - BACK + BLOCK * (j - REACH)
+        return pl.ds(pl.multiple_of(start, 64), BLOCK)
+
+    def query_rows(rank):
+        return pl.ds(pl.multiple_of(rank * rows, 64), rows)
+
+    def first(rank, scores, top_at):
+        qa = qb[query_rows(rank), :]
+        limit = rb[query_rows(rank), :] - (rank * rows - BACK)
+        top = None
+        for j in range(REACH + 2):
+            x = lax.dot_general(
+                qa, kb[key_rows(rank, j), :], (((1,), (1,)), ((), ())), preferred_element_type=jnp.float32
+            )
+            left, right = x[:, :D], x[:, D:]
+            if j >= REACH:
+                offset = (j - REACH) * BLOCK
+                left = jnp.where(column + offset <= limit, left, -1e30)
+                right = jnp.where(column + (offset + D) <= limit, right, -1e30)
+            scores[j, :, :D] = left
+            scores[j, :, D:] = right
+            larger = jnp.maximum(left, right)
+            top = larger if top is None else jnp.maximum(top, larger)
+        tops[top_at] = jnp.broadcast_to(jnp.max(top, axis=1, keepdims=True), (rows, D))
+
+    def second(rank, scores, top_at):
+        top = tops[top_at][:, :1]
+        total = jnp.zeros((rows, 2 * D), jnp.float32)
+        for j in range(REACH + 2):
+            p = jnp.exp2((scores[j] - top) * factor).astype(jnp.bfloat16)
+            total = total + jnp.dot(p, vb[key_rows(rank, j), :], preferred_element_type=jnp.float32)
+        ob[query_rows(rank), :] = (total[:, :D] / total[:, D:]).astype(jnp.bfloat16)
+
+    first(me, sa, 0)
+
+    def both(i, held, other, at):
+        send(2, i + 1).wait_recv()
+        first(behind(i + 1), other, 1 - at)
+        second(behind(i), held, at)
+
+    def pair(h, carry):
+        both(2 * h, sa, sb, 0)
+
+        @pl.when(h > 0)
         def _():
-            send(2, i).wait_recv()
-
-        rank = behind(i)
-        q0 = pl.multiple_of(rank * rows, 64)
-        count = jnp.minimum((3 * rank + 2) // 4, REACH)
-        base = front + q0 - BACK - BLOCK * count
-        qa = qb[pl.ds(q0, rows), :]
-
-        def score(j):
-            kj = kb[pl.ds(pl.multiple_of(base + BLOCK * j, 64), BLOCK), :]
-            return lax.dot_general(qa, kj, (((1,), (1,)), ((), ())), preferred_element_type=jnp.float32)
-
-        def first(j, top):
-            x = score(j)
-            sb[j] = x
-            return jnp.maximum(top, jnp.maximum(x[:, :D], x[:, D:]))
-
-        top = lax.fori_loop(0, count, first, jnp.full((rows, D), -3e38, jnp.float32))
-        limit = rb[pl.ds(q0, rows), :] - (q0 - BACK)
-        column = lax.broadcasted_iota(jnp.int32, (rows, D), 1)
-        for part in range(2):
-            x = score(count + part)
-            for half in range(2):
-                xh = x[:, half * D : (half + 1) * D]
-                xh = jnp.where(column + (part * BLOCK + half * D) <= limit, xh, -1e30)
-                sb[count + part, :, half * D : (half + 1) * D] = xh
-                top = jnp.maximum(top, xh)
-        top = jnp.max(top, axis=1, keepdims=True)
-
-        def second(j, total):
-            p = jnp.exp2((sb[j] - top) * factor).astype(jnp.bfloat16)
-            vj = vb[pl.ds(pl.multiple_of(base + BLOCK * j, 64), BLOCK), :]
-            return total + jnp.dot(p, vj, preferred_element_type=jnp.float32)
-
-        total = lax.fori_loop(0, count + 2, second, jnp.zeros((rows, 2 * D), jnp.float32))
-        ob[pl.ds(q0, rows), :] = (total[:, :D] / total[:, D:]).astype(jnp.bfloat16)
-
-        @pl.when(i > 0)
-        def _():
-            answer(i, rank).start()
-
-        @pl.when(i == 0)
+            answer(2 * h, behind(2 * h)).start()
+
+        @pl.when(h == 0)
         def _():
             keep().start()
 
+        both(2 * h + 1, sb, sa, 1)
+        answer(2 * h + 1, behind(2 * h + 1)).start()
         return carry
 
-    lax.fori_loop(0, n, chunk, 0)
+    lax.fori_loop(0, n // 2 - 1, pair, 0)
+    both(n - 2, sa, sb, 0)
+    answer(n - 2, behind(n - 2)).start()
+    second(behind(n - 1), sb, 1)
+    answer(n - 1, behind(n - 1)).start()
 
     keep().wait()
     for i in range(1, n):
@@ -191,7 +203,7 @@
         rows, width = queries.shape
         slab = doc_ids.shape[0]
         spans = span_lo.shape[0]
-        padded = 192 + slab + 256
+        padded = BACK + BLOCK * REACH + slab + BLOCK
         bf16, f32, i32 = jnp.bfloat16, jnp.float32, jnp.int32
         return pl.pallas_call(
             functools.partial(kernel, nc, nt),
@@ -205,6 +217,8 @@
                 pltpu.VMEM((slab, D), i32),
                 pltpu.VMEM((slab, D), bf16),
                 pltpu.VMEM((REACH + 2, rows, BLOCK), f32),
+                pltpu.VMEM((REACH + 2, rows, BLOCK), f32),
+                pltpu.VMEM((2, rows, D), f32),
                 pltpu.VMEM((slab // D, D), i32),
                 pltpu.SMEM((spans,), i32),
                 pltpu.SMEM((spans,), i32),

time: 77.7 us -> 49.6 us (0.64)
  Pallas kernels: 75.4 us -> 47.3 us
    pallas_call x1, Pallas kernels: 75.4 us -> 47.3 us  [step(): pl.pallas_call(functools.partial(kernel, nc, nt), out_shape=jax.ShapeDtyp...]
where the time goes in v2:
time: 49.6 us; the launch traced here: 49.4 us
  Pallas kernels  47.3 us (95%)
  local copies, waits for them, and re-layouts  2.09 us (4%)
    pallas_call x1, Pallas kernels, step(): pl.pallas_call(functools.partial(kernel, nc, nt), out_shape=jax.ShapeDtyp...  47.3 us
    unnamed x1, local copies, waits for them, and re-layouts  2.09 us

profile of v2, /device:TPU:32, one launch (start us, length us, event | category | flops | bytes accessed | tf_op | source)
XLA Modules:
  0.0 49.4 jit_solution(8211828899668247830)
XLA Ops:
  0.0 47.3 %shard_map.64 = bf16[192,2048]{1,0:T(8,128)(2,1)} custom-call(bf16[192,2048]{1,0:T(8,128)(2,1)} %q_hbm.1, bf16[192,2048]{1,0:T(8,128)(2,1)} %k_hbm.1, bf16[192,2048]{1,0:T(8,128)(2,1)} %v_hbm.1, s32[24,128]{1,0:T(8,128)} %bitcast.1, s32[6]{0:T(128)} %lo_hbm.1, s32[6]{0:T(128)} %hi_hbm.1), custom_call_target="tpu_custom_call" | custom-call | tf_op jit(solution)/shard_map/pallas_call | solution.py:208
  47.3 2.1 %copy.8 = bf16[192,2048]{1,0:T(8,128)(2,1)} copy(bf16[192,2048]{1,0:T(8,128)(2,1)} %shard_map.64) | data formatting | bytes 1572864

commit v3 on v2

--- a/solution.py
+++ b/solution.py
@@ -15,6 +15,8 @@
 REACH = 6
 FAR = float(2**20)
 
+
+ORDER = [i * 3 % 16 for i in range(16)]
 
 def kernel(
     nc, nt, q_hbm, k_hbm, v_hbm, docs_hbm, lo_hbm, hi_hbm, out,
@@ -30,10 +32,17 @@
     def device(rank):
         return {"context": rank // nt, "tensor": rank % nt}
 
+    def offset(i):
+        if isinstance(i, int):
+            return ORDER[i]
+        return sum(jnp.where(i == k, ORDER[k], 0) for k in range(n))
+
     def ahead(i):
+        i = offset(i)
         return ((c + i // nt) % nc) * nt + (t + i % nt) % nt
 
     def behind(i):
+        i = offset(i)
         return ((c + nc - i // nt) % nc) * nt + (t + nt - i % nt) % nt
 
     barrier = pltpu.get_barrier_semaphore()
@@ -70,13 +79,13 @@
         pltpu.make_async_copy(lo_hbm, lo, lsem.at[4]),
         pltpu.make_async_copy(hi_hbm, hi, lsem.at[5]),
     ]
-    for a in range(3):
+    for i in range(1, n):
+        send(0, i).start()
+    for copy in small + [own(a) for a in range(3)]:
+        copy.start()
+    for a in (1, 2):
         for i in range(1, n):
             send(a, i).start()
-        own(a).start()
-        if a == 0:
-            for copy in small:
-                copy.start()
     for copy in small:
         copy.wait()
 
@@ -98,10 +107,12 @@
         vb[start : start + count, :D] = jnp.zeros((count, D), jnp.bfloat16)
     vb[:, D:] = jnp.ones((vb.shape[0], D), jnp.bfloat16)
 
-    for a in range(2):
+    def arrive(a):
         own(a).wait()
         for i in range(1, n):
             send(a, i).wait_recv()
+
+    arrive(0)
     own(2).wait()
 
     factor = LOG2E / D**0.5
@@ -158,6 +169,7 @@
         ob[query_rows(rank), :] = (total[:, :D] / total[:, D:]).astype(jnp.bfloat16)
 
     first(me, sa, 0)
+    arrive(1)
 
     def both(i, held, other, at):
         send(2, i + 1).wait_recv()
@@ -205,11 +217,12 @@
         spans = span_lo.shape[0]
         padded = BACK + BLOCK * REACH + slab + BLOCK
         bf16, f32, i32 = jnp.bfloat16, jnp.float32, jnp.int32
+        arrays = (queries, keys, values, doc_ids.reshape(slab // D, D), span_lo, span_hi)
         return pl.pallas_call(
             functools.partial(kernel, nc, nt),
-            out_shape=jax.ShapeDtypeStruct((rows, width), bf16),
+            out_shape=pltpu.VMEM((rows, width), bf16),
             in_specs=[pl.BlockSpec(memory_space=pltpu.HBM)] * 6,
-            out_specs=pl.BlockSpec(memory_space=pltpu.HBM),
+            out_specs=pl.BlockSpec(memory_space=pltpu.VMEM),
             scratch_shapes=[
                 pltpu.VMEM((slab, 2 * D), bf16),
                 pltpu.VMEM((padded, 2 * D), bf16),
@@ -229,9 +242,9 @@
                 pltpu.SemaphoreType.DMA((7,)),
             ],
             compiler_params=pltpu.CompilerParams(
-                collective_id=0, has_side_effects=True, vmem_limit_bytes=63 << 20
+                collective_id=0, has_side_effects=True, vmem_limit_bytes=60 << 20
             ),
-        )(queries, keys, values, doc_ids.reshape(slab // D, D), span_lo, span_hi)
+        )(*[pltpu.with_memory_space_constraint(x, pltpu.HBM) for x in arrays])
 
     rows = P(("dp", "context", "tensor"), None)
     return jax.shard_map(

time: 49.6 us -> 47.5 us (0.958)
  local copies, waits for them, and re-layouts: 2.09 us -> 0.88 us
  Pallas kernels: 47.3 us -> 46.4 us
    unnamed x1, local copies, waits for them, and re-layouts: 2.09 us -> 0.88 us
    pallas_call x1, Pallas kernels: 47.3 us -> 46.4 us  [step(): pl.pallas_call(functools.partial(kernel, nc, nt), out_shape=pltpu.VMEM((r...]
where the time goes in v3:
time: 47.5 us; the launch traced here: 47.3 us
  Pallas kernels  46.4 us (98%)
  local copies, waits for them, and re-layouts  0.88 us (2%)
    pallas_call x1, Pallas kernels, step(): pl.pallas_call(functools.partial(kernel, nc, nt), out_shape=pltpu.VMEM((r...  46.4 us

profile of v3, /device:TPU:32, one launch (start us, length us, event | category | flops | bytes accessed | tf_op | source)
XLA Modules:
  0.0 47.3 jit_solution(14455086362078220716)
XLA Ops:
  0.0 46.4 %shard_map.64 = bf16[192,2048]{1,0:T(8,128)(2,1)S(1)} custom-call(bf16[192,2048]{1,0:T(8,128)(2,1)} %q_hbm.1, bf16[192,2048]{1,0:T(8,128)(2,1)} %k_hbm.1, bf16[192,2048]{1,0:T(8,128)(2,1)} %v_hbm.1, s32[24,128]{1,0:T(8,128)} %bitcast.1, s32[6]{0:T(128)} %lo_hbm.1, s32[6]{0:T(128)} %hi_hbm.1), custom_call_target="tpu_custom_call" | custom-call | tf_op jit(solution)/shard_map/pallas_call | solution.py:221
  46.5 0.9 %copy.8 = bf16[192,2048]{1,0:T(8,128)(2,1)} copy(bf16[192,2048]{1,0:T(8,128)(2,1)S(1)} %shard_map.64) | data formatting | bytes 1572864

commit v4 on v3

--- a/solution.py
+++ b/solution.py
@@ -16,11 +16,14 @@
 FAR = float(2**20)
 
 
-ORDER = [i * 3 % 16 for i in range(16)]
+ORDER = (0, 10, 1, 4, 3, 12, 9, 6, 11, 14, 2, 8, 5, 15, 7, 13)
+
+EARLY = 8
+
 
 def kernel(
     nc, nt, q_hbm, k_hbm, v_hbm, docs_hbm, lo_hbm, hi_hbm, out,
-    qb, kb, vb, rb, ob, sa, sb, tops, docs, lo, hi, ssem, rsem, osend, orecv, lsem,
+    qb, kb, vb, rb, ob, pb, sa, sb, tops, docs, lo, hi, ssem, rsem, osend, orecv, lsem,
 ):
     rows = q_hbm.shape[0]
     n = nc * nt
@@ -50,9 +53,9 @@
         pl.semaphore_signal(barrier, inc=1, device_id=device(ahead(i)), device_id_type=MESH)
     pl.semaphore_wait(barrier, n - 1)
 
-    sources = (k_hbm, v_hbm, q_hbm)
-    buffers = (kb, vb, qb)
-    offsets = (front, front, 0)
+    sources = (k_hbm, q_hbm, v_hbm)
+    buffers = (kb, qb, vb)
+    offsets = (front, 0, front)
 
     def columns(rank):
         return pl.ds(pl.multiple_of(rank * D, D), D)
@@ -83,9 +86,12 @@
         send(0, i).start()
     for copy in small + [own(a) for a in range(3)]:
         copy.start()
-    for a in (1, 2):
-        for i in range(1, n):
-            send(a, i).start()
+    for i in range(1, EARLY + 1):
+        send(1, i).start()
+    for i in range(1, n):
+        send(2, i).start()
+    for i in range(EARLY + 1, n):
+        send(1, i).start()
     for copy in small:
         copy.wait()
 
@@ -113,7 +119,7 @@
             send(a, i).wait_recv()
 
     arrive(0)
-    own(2).wait()
+    own(1).wait()
 
     factor = LOG2E / D**0.5
 
@@ -160,7 +166,21 @@
             top = larger if top is None else jnp.maximum(top, larger)
         tops[top_at] = jnp.broadcast_to(jnp.max(top, axis=1, keepdims=True), (rows, D))
 
-    def second(rank, scores, top_at):
+    def second(i, scores, top_at):
+        top = tops[top_at][:, :1]
+        for j in range(REACH + 2):
+            pb[i, :, j * BLOCK : (j + 1) * BLOCK] = jnp.exp2((scores[j] - top) * factor).astype(jnp.bfloat16)
+
+    def third(i):
+        rank = behind(i)
+        start = pl.multiple_of(front + rank * rows - BACK - BLOCK * REACH, 64)
+        total = jnp.dot(
+            pb[i], vb[pl.ds(start, (REACH + 2) * BLOCK), :], preferred_element_type=jnp.float32
+        )
+        ob[query_rows(rank), :] = (total[:, :D] / total[:, D:]).astype(jnp.bfloat16)
+
+    def whole(i, scores, top_at):
+        rank = behind(i)
         top = tops[top_at][:, :1]
         total = jnp.zeros((rows, 2 * D), jnp.float32)
         for j in range(REACH + 2):
@@ -168,34 +188,49 @@
             total = total + jnp.dot(p, vb[key_rows(rank, j), :], preferred_element_type=jnp.float32)
         ob[query_rows(rank), :] = (total[:, :D] / total[:, D:]).astype(jnp.bfloat16)
 
+    def reply(i):
+        answer(i, behind(i)).start()
+
     first(me, sa, 0)
-    arrive(1)
-
-    def both(i, held, other, at):
-        send(2, i + 1).wait_recv()
-        first(behind(i + 1), other, 1 - at)
-        second(behind(i), held, at)
-
-    def pair(h, carry):
-        both(2 * h, sa, sb, 0)
-
-        @pl.when(h > 0)
-        def _():
-            answer(2 * h, behind(2 * h)).start()
-
-        @pl.when(h == 0)
-        def _():
-            keep().start()
-
-        both(2 * h + 1, sb, sa, 1)
-        answer(2 * h + 1, behind(2 * h + 1)).start()
+
+    def before(h, carry):
+        for e, held, other in ((0, sa, sb), (1, sb, sa)):
+            i = 2 * h + e
+            send(1, i + 1).wait_recv()
+            first(behind(i + 1), other, 1 - e)
+            second(i, held, e)
         return carry
 
-    lax.fori_loop(0, n // 2 - 1, pair, 0)
-    both(n - 2, sa, sb, 0)
-    answer(n - 2, behind(n - 2)).start()
-    second(behind(n - 1), sb, 1)
-    answer(n - 1, behind(n - 1)).start()
+    lax.fori_loop(0, EARLY // 2, before, 0)
+    second(EARLY, sa, 0)
+    arrive(2)
+
+    def product(h, carry):
+        third(2 * h + 1)
+        third(2 * h + 2)
+        reply(2 * h + 1)
+        reply(2 * h + 2)
+        return carry
+
+    lax.fori_loop(0, EARLY // 2, product, 0)
+
+    send(1, EARLY + 1).wait_recv()
+    first(behind(EARLY + 1), sb, 1)
+    third(0)
+    keep().start()
+
+    def after(h, carry):
+        for e, held, other in ((1, sb, sa), (0, sa, sb)):
+            i = EARLY + 1 + 2 * h + (1 - e)
+            send(1, i + 1).wait_recv()
+            first(behind(i + 1), other, 1 - e)
+            whole(i, held, e)
+            reply(i)
+        return carry
+
+    lax.fori_loop(0, (n - 2 - EARLY) // 2, after, 0)
+    whole(n - 1, sb, 1)
+    reply(n - 1)
 
     keep().wait()
     for i in range(1, n):
@@ -229,6 +264,7 @@
                 pltpu.VMEM((padded, 2 * D), bf16),
                 pltpu.VMEM((slab, D), i32),
                 pltpu.VMEM((slab, D), bf16),
+                pltpu.VMEM((n, rows, (REACH + 2) * BLOCK), bf16),
                 pltpu.VMEM((REACH + 2, rows, BLOCK), f32),
                 pltpu.VMEM((REACH + 2, rows, BLOCK), f32),
                 pltpu.VMEM((2, rows, D), f32),

time: 47.5 us -> 46.1 us (0.971)
  Pallas kernels: 46.4 us -> 44.9 us
    pallas_call x1, Pallas kernels: 46.4 us -> 44.9 us  [step(): pl.pallas_call(functools.partial(kernel, nc, nt), out_shape=pltpu.VMEM((r...]
where the time goes in v4:
time: 46.1 us; the launch traced here: 45.8 us
  Pallas kernels  44.9 us (97%)
  local copies, waits for them, and re-layouts  0.88 us (2%)
    pallas_call x1, Pallas kernels, step(): pl.pallas_call(functools.partial(kernel, nc, nt), out_shape=pltpu.VMEM((r...  44.9 us

profile of v4, /device:TPU:32, one launch (start us, length us, event | category | flops | bytes accessed | tf_op | source)
XLA Modules:
  0.0 45.8 jit_solution(5450988987755716011)
XLA Ops:
  0.0 44.9 %shard_map.64 = bf16[192,2048]{1,0:T(8,128)(2,1)S(1)} custom-call(bf16[192,2048]{1,0:T(8,128)(2,1)} %q_hbm.1, bf16[192,2048]{1,0:T(8,128)(2,1)} %k_hbm.1, bf16[192,2048]{1,0:T(8,128)(2,1)} %v_hbm.1, s32[24,128]{1,0:T(8,128)} %bitcast.1, s32[6]{0:T(128)} %lo_hbm.1, s32[6]{0:T(128)} %hi_hbm.1), custom_call_target="tpu_custom_call" | custom-call | tf_op jit(solution)/shard_map/pallas_call | solution.py:256
  44.9 0.9 %copy.8 = bf16[192,2048]{1,0:T(8,128)(2,1)} copy(bf16[192,2048]{1,0:T(8,128)(2,1)S(1)} %shard_map.64) | data formatting | bytes 1572864

commit v5 on v4

--- a/solution.py
+++ b/solution.py
@@ -13,7 +13,6 @@
 BLOCK = 256
 BACK = 64
 REACH = 6
-FAR = float(2**20)
 
 
 ORDER = (0, 10, 1, 4, 3, 12, 9, 6, 11, 14, 2, 8, 5, 15, 7, 13)
@@ -23,7 +22,7 @@
 
 def kernel(
     nc, nt, q_hbm, k_hbm, v_hbm, docs_hbm, lo_hbm, hi_hbm, out,
-    qb, kb, vb, rb, ob, pb, sa, sb, tops, docs, lo, hi, ssem, rsem, osend, orecv, lsem,
+    qb, kb, vb, rs, rb, ob, pb, sa, sb, tops, docs, lo, hi, ssem, rsem, osend, orecv, lsem,
 ):
     rows = q_hbm.shape[0]
     n = nc * nt
@@ -31,26 +30,35 @@
     front = BACK + BLOCK * REACH
     c, t = lax.axis_index("context"), lax.axis_index("tensor")
     me = c * nt + t
-
-    def device(rank):
-        return {"context": rank // nt, "tensor": rank % nt}
+    contexts = [lax.rem(c + d, nc) for d in range(nc)]
+    tensors = [lax.rem(t + d, nt) for d in range(nt)]
 
     def offset(i):
         if isinstance(i, int):
             return ORDER[i]
         return sum(jnp.where(i == k, ORDER[k], 0) for k in range(n))
 
+    def place_of(context, tensor):
+        return context * nt + tensor, {"context": context, "tensor": tensor}
+
     def ahead(i):
-        i = offset(i)
-        return ((c + i // nt) % nc) * nt + (t + i % nt) % nt
+        o = offset(i)
+        if isinstance(i, int):
+            return place_of(contexts[o // nt], tensors[o % nt])
+        return place_of(lax.rem(c + lax.div(o, nt), nc), lax.rem(t + lax.rem(o, nt), nt))
+
+    def back(i):
+        o = offset(i)
+        if isinstance(i, int):
+            return place_of(contexts[-(o // nt) % nc], tensors[-(o % nt) % nt])
+        return place_of(lax.rem(c + nc - lax.div(o, nt), nc), lax.rem(t + nt - lax.rem(o, nt), nt))
 
     def behind(i):
-        i = offset(i)
-        return ((c + nc - i // nt) % nc) * nt + (t + nt - i % nt) % nt
+        return back(i)[0]
 
     barrier = pltpu.get_barrier_semaphore()
     for i in range(1, n):
-        pl.semaphore_signal(barrier, inc=1, device_id=device(ahead(i)), device_id_type=MESH)
+        pl.semaphore_signal(barrier, inc=1, device_id=ahead(i)[1], device_id_type=MESH)
     pl.semaphore_wait(barrier, n - 1)
 
     sources = (k_hbm, q_hbm, v_hbm)
@@ -64,13 +72,13 @@
         return buffers[a].at[pl.ds(pl.multiple_of(offsets[a] + rank * rows, 64), rows), pl.ds(0, D)]
 
     def send(a, i):
-        to = ahead(i)
+        to, device = ahead(i)
         return pltpu.make_async_remote_copy(
             src_ref=sources[a].at[:, columns(to)],
             dst_ref=place(a, me),
             send_sem=ssem.at[a, i],
             recv_sem=rsem.at[a, i],
-            device_id=device(to),
+            device_id=device,
             device_id_type=MESH,
         )
 
@@ -95,21 +103,22 @@
     for copy in small:
         copy.wait()
 
-    lane = lax.broadcasted_iota(jnp.int32, (D, D), 1)
+    def below(d):
+        return jnp.sum(jnp.where(docs[...] < d, 1, 0), axis=(0, 1), keepdims=True)
+
+    second_doc, third_doc = below(1), below(2)
     row = lax.broadcasted_iota(jnp.int32, (D, D), 0)
     for b in range(slab // D):
         doc = jnp.transpose(jnp.broadcast_to(docs[b : b + 1, :], (D, D)))
-        same = doc == lane
-        kb[front + b * D : front + (b + 1) * D, D:] = jnp.where(same, 1.0, 0.0).astype(jnp.bfloat16)
-        qb[b * D : (b + 1) * D, D:] = jnp.where(same | (lane > 2), 0.0, -FAR).astype(jnp.bfloat16)
         at = row + b * D
         last = at
         for s in range(lo_hbm.shape[0]):
             last = jnp.where((at >= lo[s]) & (at < hi[s]), hi[s] - 1, last)
-        rb[b * D : (b + 1) * D, :] = last
+        end = jnp.where(doc == 0, second_doc, jnp.where(doc == 1, third_doc, slab))
+        rb[b * D : (b + 1) * D, :] = jnp.minimum(last, end - 1)
+        rs[b * D : (b + 1) * D, :] = jnp.where(doc == 0, 0, jnp.where(doc == 1, second_doc, third_doc))
     for start, count in ((0, front), (front + slab, BLOCK)):
-        kb[start : start + count, :D] = jnp.zeros((count, D), jnp.bfloat16)
-        kb[start : start + count, D:] = jnp.ones((count, D), jnp.bfloat16)
+        kb[start : start + count, :] = jnp.zeros((count, D), jnp.bfloat16)
         vb[start : start + count, :D] = jnp.zeros((count, D), jnp.bfloat16)
     vb[:, D:] = jnp.ones((vb.shape[0], D), jnp.bfloat16)
 
@@ -123,13 +132,14 @@
 
     factor = LOG2E / D**0.5
 
-    def answer(i, rank):
+    def answer(i):
+        rank, device = back(i)
         return pltpu.make_async_remote_copy(
             src_ref=ob.at[pl.ds(pl.multiple_of(rank * rows, 64), rows), :],
             dst_ref=out.at[:, columns(me)],
             send_sem=osend.at[i],
             recv_sem=orecv.at[i],
-            device_id=device(rank),
+            device_id=device,
             device_id_type=MESH,
         )
 
@@ -149,17 +159,17 @@
 
     def first(rank, scores, top_at):
         qa = qb[query_rows(rank), :]
-        limit = rb[query_rows(rank), :] - (rank * rows - BACK)
+        origin = rank * rows - BACK - BLOCK * REACH
+        least, limit = rs[query_rows(rank), :] - origin, rb[query_rows(rank), :] - origin
         top = None
         for j in range(REACH + 2):
             x = lax.dot_general(
                 qa, kb[key_rows(rank, j), :], (((1,), (1,)), ((), ())), preferred_element_type=jnp.float32
             )
             left, right = x[:, :D], x[:, D:]
-            if j >= REACH:
-                offset = (j - REACH) * BLOCK
-                left = jnp.where(column + offset <= limit, left, -1e30)
-                right = jnp.where(column + (offset + D) <= limit, right, -1e30)
+            near, far = column + j * BLOCK, column + (j * BLOCK + D)
+            left = jnp.where((near >= least) & (near <= limit) if j >= REACH else near >= least, left, -1e30)
+            right = jnp.where((far >= least) & (far <= limit) if j >= REACH else far >= least, right, -1e30)
             scores[j, :, :D] = left
             scores[j, :, D:] = right
             larger = jnp.maximum(left, right)
@@ -189,7 +199,7 @@
         ob[query_rows(rank), :] = (total[:, :D] / total[:, D:]).astype(jnp.bfloat16)
 
     def reply(i):
-        answer(i, behind(i)).start()
+        answer(i).start()
 
     first(me, sa, 0)
 
@@ -216,8 +226,6 @@
 
     send(1, EARLY + 1).wait_recv()
     first(behind(EARLY + 1), sb, 1)
-    third(0)
-    keep().start()
 
     def after(h, carry):
         for e, held, other in ((1, sb, sa), (0, sa, sb)):
@@ -231,15 +239,17 @@
     lax.fori_loop(0, (n - 2 - EARLY) // 2, after, 0)
     whole(n - 1, sb, 1)
     reply(n - 1)
+    third(0)
+    keep().start()
 
     keep().wait()
-    for i in range(1, n):
-        answer(i, behind(i)).wait_recv()
-    for i in range(1, n):
-        answer(i, behind(i)).wait_send()
     for a in range(3):
         for i in range(1, n):
             send(a, i).wait_send()
+    for i in range(1, n):
+        answer(i).wait_send()
+    for i in range(1, n):
+        answer(i).wait_recv()
 
 
 def solution(mesh):
@@ -259,9 +269,10 @@
             in_specs=[pl.BlockSpec(memory_space=pltpu.HBM)] * 6,
             out_specs=pl.BlockSpec(memory_space=pltpu.VMEM),
             scratch_shapes=[
-                pltpu.VMEM((slab, 2 * D), bf16),
+                pltpu.VMEM((slab, D), bf16),
+                pltpu.VMEM((padded, D), bf16),
                 pltpu.VMEM((padded, 2 * D), bf16),
-                pltpu.VMEM((padded, 2 * D), bf16),
+                pltpu.VMEM((slab, D), i32),
                 pltpu.VMEM((slab, D), i32),
                 pltpu.VMEM((slab, D), bf16),
                 pltpu.VMEM((n, rows, (REACH + 2) * BLOCK), bf16),

time: 46.1 us -> 45.1 us (0.978)
  Pallas kernels: 44.9 us -> 43.7 us
    pallas_call x1, Pallas kernels: 44.9 us -> 43.7 us  [step(): pl.pallas_call(functools.partial(kernel, nc, nt), out_shape=pltpu.VMEM((r...]
where the time goes in v5:
time: 45.1 us; the launch traced here: 44.6 us
  Pallas kernels  43.7 us (97%)
  local copies, waits for them, and re-layouts  0.88 us (2%)
    pallas_call x1, Pallas kernels, step(): pl.pallas_call(functools.partial(kernel, nc, nt), out_shape=pltpu.VMEM((r...  43.7 us

profile of v5, /device:TPU:32, one launch (start us, length us, event | category | flops | bytes accessed | tf_op | source)
XLA Modules:
  0.0 44.6 jit_solution(16193665727516770464)
XLA Ops:
  0.0 43.7 %shard_map.64 = bf16[192,2048]{1,0:T(8,128)(2,1)S(1)} custom-call(bf16[192,2048]{1,0:T(8,128)(2,1)} %q_hbm.1, bf16[192,2048]{1,0:T(8,128)(2,1)} %k_hbm.1, bf16[192,2048]{1,0:T(8,128)(2,1)} %v_hbm.1, s32[24,128]{1,0:T(8,128)} %bitcast.1, s32[6]{0:T(128)} %lo_hbm.1, s32[6]{0:T(128)} %hi_hbm.1), custom_call_target="tpu_custom_call" | custom-call | tf_op jit(solution)/shard_map/pallas_call | solution.py:266
  43.8 0.9 %copy.8 = bf16[192,2048]{1,0:T(8,128)(2,1)} copy(bf16[192,2048]{1,0:T(8,128)(2,1)S(1)} %shard_map.64) | data formatting | bytes 1572864

commit v6 on v5

--- a/solution.py
+++ b/solution.py
@@ -17,7 +17,7 @@
 
 ORDER = (0, 10, 1, 4, 3, 12, 9, 6, 11, 14, 2, 8, 5, 15, 7, 13)
 
-EARLY = 8
+EARLY = 4
 
 
 def kernel(

time: 45.1 us -> 45 us (level)
  no operation moved by 1% of the time
where the time goes in v6:
time: 45 us; the launch traced here: 44.4 us
  Pallas kernels  43.5 us (97%)
  local copies, waits for them, and re-layouts  0.88 us (2%)
    pallas_call x1, Pallas kernels, step(): pl.pallas_call(functools.partial(kernel, nc, nt), out_shape=pltpu.VMEM((r...  43.5 us

profile of v6, /device:TPU:32, one launch (start us, length us, event | category | flops | bytes accessed | tf_op | source)
XLA Modules:
  0.0 44.4 jit_solution(15149097329448311971)
XLA Ops:
  0.0 43.5 %shard_map.64 = bf16[192,2048]{1,0:T(8,128)(2,1)S(1)} custom-call(bf16[192,2048]{1,0:T(8,128)(2,1)} %q_hbm.1, bf16[192,2048]{1,0:T(8,128)(2,1)} %k_hbm.1, bf16[192,2048]{1,0:T(8,128)(2,1)} %v_hbm.1, s32[24,128]{1,0:T(8,128)} %bitcast.1, s32[6]{0:T(128)} %lo_hbm.1, s32[6]{0:T(128)} %hi_hbm.1), custom_call_target="tpu_custom_call" | custom-call | tf_op jit(solution)/shard_map/pallas_call | solution.py:266
  43.5 0.9 %copy.8 = bf16[192,2048]{1,0:T(8,128)(2,1)} copy(bf16[192,2048]{1,0:T(8,128)(2,1)S(1)} %shard_map.64) | data formatting | bytes 1572864
